TPU v7x, 256 devices: a whole 4x4x8 slice. The times are simulated.
256 devices in a mesh: section: 4 (over z_lo), seq: 64 (over z_hi, x, y, core).
Axes of the slice: x: 4, y: 4, z: 8 (z_hi: 2, z_lo: 4; z = z_hi * 4 + z_lo), core: 2. Of those that a mesh axis runs over, the one named last changes fastest.
Arguments:
- features: bfloat16 [1536, 32, 256], P('seq'), may hold values from -6 to 6
- conv_kernels: bfloat16 [4, 3, 3, 256, 256], P('section'), may hold values from -0.125 to 0.125
- patch_weights: bfloat16 [4, 4096, 1024], P('section'), may hold values from -0.1875 to 0.1875
- positions: int32 [48], replicated, may hold values from 0 to 3840
- out_cotangent: bfloat16 [1536, 32, 256], P('seq'), may hold values from -6 to 6
Outputs:
- weight_grads: float32 [4, 4096, 1024], P('section', 'seq')
All inputs are finite; a program needn't handle non-finite values.
Results may differ from a plain program's by a relative error of at most 0.027.
Values may be sent and summed in bfloat16 or wider, within the bound.
No kernel may reach another device: no remote copies, remote signals or barrier semaphores. Data moves between devices by JAX's collectives and lax.ppermute only.
A program may use at most 128 MiB of HBM per device.

v0:
```python
import math

import jax
import jax.numpy as jnp
from jax import lax
from jax.sharding import PartitionSpec as P

NORM_EPS = 1e-05


def shifted(value, axis, by):
    count = lax.axis_size(axis)
    pairs = [(i, i + by) for i in range(count) if 0 <= i + by < count]
    return lax.ppermute(value, axis, pairs)


def with_halo(value, sides, width):
    for axis, dim in sides:
        count, length = (lax.axis_size(axis), value.shape[dim])
        up = [(i, (i + 1) % count) for i in range(count)]
        down = [(j, i) for i, j in up]
        last = lax.slice_in_dim(value, length - width, length, axis=dim)
        initial = lax.slice_in_dim(value, 0, width, axis=dim)
        before = lax.ppermute(last, axis, up)
        after = lax.ppermute(initial, axis, down)
        value = jnp.concatenate([before, value, after], axis=dim)
    return value


def patchify(field):
    count, side, channels = field.shape
    blocks = field.reshape(count // 2, 2, side // 2, 2, channels).transpose(0, 2, 1, 3, 4)
    return blocks.reshape(count // 2 * (side // 2), 4 * channels)


def unpatchify(tokens, count, side):
    channels = tokens.shape[1] // 4
    blocks = tokens.reshape(count // 2, side // 2, 2, 2, channels).transpose(0, 2, 1, 3, 4)
    return blocks.reshape(count, side, channels)


def normed(tokens):
    scale = lax.rsqrt(jnp.mean(tokens * tokens, axis=-1, keepdims=True) + NORM_EPS)
    return (tokens * scale, scale)


def silu_slope(value):
    sigma = jax.nn.sigmoid(value)
    return sigma * (1.0 + value * (1.0 - sigma))


def norm_back(grad_out, tokens):
    normal, scale = normed(tokens)
    inner = grad_out * silu_slope(normal)
    return scale * (inner - normal * jnp.mean(inner * normal, axis=-1, keepdims=True))


def position_code(places, width):
    half = width // 2
    rates = jnp.exp(jnp.arange(half, dtype=jnp.float32) * (-math.log(10000.0) / half))
    angle = places.astype(jnp.float32)[:, None] * rates[None, :]
    return jnp.concatenate([jnp.sin(angle), jnp.cos(angle)], axis=1)


def stacked_taps(upper, middle, lower):
    pieces = []
    side = middle.shape[1]
    for part in (upper, middle, lower):
        wide = jnp.pad(part, ((0, 0), (1, 1), (0, 0)))
        pieces += [wide[:, 0:side], wide[:, 1 : side + 1], wide[:, 2 : side + 2]]
    return jnp.concatenate(pieces, axis=2)


def apply_taps(taps, kernel):
    count, side, depth = taps.shape
    result = jnp.dot(taps.reshape(count * side, depth), kernel, preferred_element_type=jnp.float32)
    return result.reshape(count, side, kernel.shape[1])


def pass_on(current, carried):
    return (shifted(current, "section", 1), carried)


def pass_back(current):
    return shifted(current, "section", -1)


def on_device(features, conv_kernels, patch_weights, positions, out_cotangent):
    count_rows, side, channels = features.shape
    weight = patch_weights[0]
    width = weight.shape[0]
    section = lax.axis_index("section")
    place = lax.axis_index("seq")
    image_count = positions.shape[0]
    kernel = conv_kernels[0]
    ahead = kernel.reshape(9 * channels, channels)
    behind = jnp.transpose(kernel[::-1, ::-1], (0, 1, 3, 2)).reshape(9 * channels, channels)
    half_side = side // 2
    row_index = place * count_rows + lax.iota(jnp.int32, count_rows) + half_side
    keep_upper = (row_index % side != 0)[:, None, None]
    keep_lower = (row_index % side != side - 1)[:, None, None]
    count_tokens = count_rows // 2 * (side // 2)
    grid_zero = jnp.zeros((count_rows, side, channels), jnp.float32)
    token_zero = jnp.zeros((count_tokens, width), jnp.bfloat16)
    pair_rows = place * count_rows + 2 * lax.iota(jnp.int32, count_rows // 2) + half_side
    owner = pair_rows // side % image_count
    image_ids = lax.iota(jnp.int32, image_count)
    begins = jnp.sum(jnp.where(owner[:, None] == image_ids[None, :], positions[None, :], 0), axis=1)
    within = pair_rows % side // 2 * (side // 2)
    places = (begins + within)[:, None] + lax.iota(jnp.int32, side // 2)[None, :]

    def convolve(field, taps_kernel, active):
        padded = with_halo(field, (("seq", 0),), 1)

        def compute(source):
            upper = jnp.where(keep_upper, source[0:count_rows], 0)
            lower = jnp.where(keep_lower, source[2 : count_rows + 2], 0)
            return apply_taps(stacked_taps(upper, source[1 : count_rows + 1], lower), taps_kernel)

        return lax.cond(active, compute, lambda source: grid_zero, padded)

    def embed_first(field):
        embedded = jnp.dot(patchify(field), weight.T, preferred_element_type=jnp.float32)
        return (embedded + position_code(places.reshape(-1), width)).astype(jnp.bfloat16)

    def lift(tokens):
        normal, _ = normed(tokens.astype(jnp.float32))
        active = jax.nn.silu(normal).astype(jnp.bfloat16)
        lifted = unpatchify(
            jnp.dot(active, weight, preferred_element_type=jnp.float32), count_rows, side
        )
        return (active, lifted)

    def lift_last(pair):
        active, lifted = lift(pair[0])
        return (active, lifted + pair[1].astype(jnp.float32))

    def lift_zero(operand):
        return (token_zero, grid_zero)

    def descend(pair):
        grad_out = jnp.dot(pair[0], weight.T, preferred_element_type=jnp.float32)
        return norm_back(grad_out, pair[1].astype(jnp.float32)).astype(jnp.bfloat16)

    skip_field = convolve(features, ahead, section == 0).astype(jnp.bfloat16)
    first_tokens = lax.cond(section == 0, embed_first, lambda field: token_zero, skip_field)
    first_recv, carried = pass_on(first_tokens, skip_field)
    first_act, first_lift = lax.cond(section == 1, lift, lift_zero, first_recv)
    first_input = jax.nn.silu(first_lift).astype(jnp.bfloat16)
    second_field = convolve(first_input, ahead, section == 1).astype(jnp.bfloat16)
    second_recv, carried = pass_on(second_field, carried)
    second_input = jax.nn.silu(second_recv.astype(jnp.float32)).astype(jnp.bfloat16)
    third_field = convolve(second_input, ahead, section == 2).astype(jnp.bfloat16)
    third_patch = patchify(third_field)
    third_tokens = lax.cond(
        section == 2,
        lambda patches: jnp.dot(patches, weight.T, preferred_element_type=jnp.float32).astype(
            jnp.bfloat16
        ),
        lambda patches: token_zero,
        third_patch,
    )
    third_recv, carried = pass_on(third_tokens, carried)
    skip_last = shifted(skip_field, "section", 3)
    last_act, last_lift = lax.cond(section == 3, lift_last, lift_zero, (third_recv, skip_last))
    last_grad = (convolve(out_cotangent, behind, section == 3) * silu_slope(last_lift)).astype(
        jnp.bfloat16
    )
    last_patch = patchify(last_grad)
    third_back = lax.cond(section == 3, descend, lambda pair: token_zero, (last_patch, third_recv))
    third_given = pass_back(third_back)
    third_lift = lax.cond(
        section == 2,
        lambda tokens: unpatchify(
            jnp.dot(tokens, weight, preferred_element_type=jnp.float32), count_rows, side
        ).astype(jnp.bfloat16),
        lambda tokens: grid_zero.astype(jnp.bfloat16),
        third_given,
    )
    second_back = (
        convolve(third_lift, behind, section == 2) * silu_slope(second_recv.astype(jnp.float32))
    ).astype(jnp.bfloat16)
    second_given = pass_back(second_back)
    first_grad = (convolve(second_given, behind, section == 1) * silu_slope(first_lift)).astype(
        jnp.bfloat16
    )
    first_patch = patchify(first_grad)
    first_back = lax.cond(section == 1, descend, lambda pair: token_zero, (first_patch, first_recv))
    first_given = pass_back(first_back)
    token_side, patch_side = lax.switch(
        section,
        [
            lambda: (first_given, patchify(skip_field)),
            lambda: (first_act, first_patch),
            lambda: (third_given, third_patch),
            lambda: (last_act, last_patch),
        ],
    )
    devices = lax.axis_size("seq")
    share = width // devices
    scale = 1.0 / math.sqrt(devices * count_tokens)
    columns = lax.slice_in_dim(token_side, 0, lax.axis_size("seq") * share, axis=1)
    summed = lax.psum_scatter(
        jnp.dot(columns.T, patch_side, preferred_element_type=jnp.float32),
        "seq",
        scatter_dimension=0,
        tiled=True,
    )
    return (summed * scale)[None]


def solution(mesh):
    in_specs = (
        P("seq", None, None),
        P("section", None, None, None, None),
        P("section", None, None),
        P(),
        P("seq", None, None),
    )
    out_specs = P("section", "seq", None)
    return jax.shard_map(
        on_device, mesh=mesh, in_specs=in_specs, out_specs=out_specs, check_vma=False
    )
```

profile of v0, /device:TPU:32, one launch (start us, length us, event | category | flops | bytes accessed | tf_op | source)
XLA Modules:
  0.0 776.2 jit_solution(16368640781196199679)
XLA Ops:
  7.3 10.4 %collective-permute-start.1 = (bf16[1,32,256]{2,1,0:T(8,128)(2,1)S(1)}, bf16[1,32,256]{2,1,0:T(8,128)(2,1)S(1)}, u32[]{:S(2)}, u32[]{:S(2)}) collective-permute-start(bf16[1,32,256]{2,1,0:T(8,128)(2,1)S(1)} %get-tuple-element.601), channel_id=1, source_target_pairs={{1,0},{2,1},{3,2},{4,3},{5,4},{6,5},{7,6},{8,7},{9,8},{10,9},{11,1... | collective-permute-start | bytes 49160 | tf_op jit(solution)/shard_map/ppermute | solution.py:25
  21.4 3.3 collective-permute-start.2
  24.7 42.7 %collective-permute-done.2 = bf16[192,4096]{1,0:T(8,128)(2,1)S(1)} collective-permute-done((bf16[192,4096]{1,0:T(8,128)(2,1)S(1)}, bf16[192,4096]{1,0:T(8,128)(2,1)S(1)}, u32[]{:S(2)}, u32[]{:S(2)}) %collective-permute-start.2) | collective-permute-done | bytes 1572896 | tf_op jit(solution)/shard_map/ppermute | solution.py:14
  67.4 12.3 %conditional.16 = (bf16[192,4096]{1,0:T(8,128)(2,1)}, f32[24,32,256]{2,1,0:T(8,128)}, f32[24,32,256]{2,1,0:T(8,128)S(1)}) conditional(s32[]{:T(128)} %convert_element_type.150, () %tuple.135, (bf16[192,4096]{1,0:T(8,128)(2,1)S(1)}, bf16[4096,1024]{1,0:T(8,128)(2,1)}) %tuple.209), branch_computations={%region_7.8_spmd, %region_8.10_spmd} | conditional | flops 1618673920 | bytes 21761048 | solution.py:148
  68.2 2.1 fusion.20
  70.3 5.7 fusion.108
  81.4 10.5 %collective-permute-start.4 = (bf16[1,32,256]{2,1,0:T(8,128)(2,1)S(1)}, bf16[1,32,256]{2,1,0:T(8,128)(2,1)S(1)}, u32[]{:S(2)}, u32[]{:S(2)}) collective-permute-start(bf16[1,32,256]{2,1,0:T(8,128)(2,1)S(1)} %get-tuple-element.599), channel_id=1, source_target_pairs={{1,0},{2,1},{3,2},{4,3},{5,4},{6,5},{7,6},{8,7},{9,8},{10,9},{11,1... | collective-permute-start | bytes 49160 | tf_op jit(solution)/shard_map/ppermute | solution.py:25
  93.4 4.0 conditional.17
  95.5 1.8 fusion.22
  97.4 1.9 collective-permute-start.5
  99.3 8.0 %collective-permute-done.5 = bf16[24,32,256]{2,1,0:T(8,128)(2,1)S(1)} collective-permute-done((bf16[24,32,256]{2,1,0:T(8,128)(2,1)}, bf16[24,32,256]{2,1,0:T(8,128)(2,1)S(1)}, u32[]{:S(2)}, u32[]{:S(2)}) %collective-permute-start.5) | collective-permute-done | bytes 393248 | tf_op jit(solution)/shard_map/ppermute | solution.py:14
  108.4 9.9 %collective-permute-start.7 = (bf16[1,32,256]{2,1,0:T(8,128)(2,1)S(1)}, bf16[1,32,256]{2,1,0:T(8,128)(2,1)S(1)}, u32[]{:S(2)}, u32[]{:S(2)}) collective-permute-start(bf16[1,32,256]{2,1,0:T(8,128)(2,1)S(1)} %get-tuple-element.597), channel_id=1, source_target_pairs={{1,0},{2,1},{3,2},{4,3},{5,4},{6,5},{7,6},{8,7},{9,8},{10,9},{11,1... | collective-permute-start | bytes 49160 | tf_op jit(solution)/shard_map/ppermute | solution.py:25
  122.8 11.3 %collective-permute-start.8 = (bf16[192,4096]{1,0:T(8,128)(2,1)}, bf16[192,4096]{1,0:T(8,128)(2,1)S(1)}, u32[]{:S(2)}, u32[]{:S(2)}) collective-permute-start(bf16[192,4096]{1,0:T(8,128)(2,1)} %copy-done.4), channel_id=1, source_target_pairs={{0,64},{64,128},{128,192},{1,65},{65,129},{129,193},{2,66},{66,130... | collective-permute-start | bytes 4718600 | tf_op jit(solution)/shard_map/ppermute | solution.py:14
  136.2 9.9 %collective-permute-start.10 = (bf16[1,32,256]{2,1,0:T(8,128)(2,1)S(1)}, bf16[1,32,256]{2,1,0:T(8,128)(2,1)}, u32[]{:S(2)}, u32[]{:S(2)}) collective-permute-start(bf16[1,32,256]{2,1,0:T(8,128)(2,1)S(1)} %get-tuple-element.595), channel_id=1, source_target_pairs={{1,0},{2,1},{3,2},{4,3},{5,4},{6,5},{7,6},{8,7},{9,8},{10,9},{11,1... | collective-permute-start | bytes 49160 | tf_op jit(solution)/shard_map/ppermute | solution.py:25
  146.1 2.4 reverse_bitcast_fusion
  148.4 2.4 copy.22
  153.4 13.6 %collective-permute-done.8 = bf16[192,4096]{1,0:T(8,128)(2,1)S(1)} collective-permute-done((bf16[192,4096]{1,0:T(8,128)(2,1)}, bf16[192,4096]{1,0:T(8,128)(2,1)S(1)}, u32[]{:S(2)}, u32[]{:S(2)}) %collective-permute-start.8) | collective-permute-done | bytes 1572896 | tf_op jit(solution)/shard_map/ppermute | solution.py:14
  168.7 2.1 multiply_convert_fusion.1
  173.1 2.0 reshape.279
  176.4 8.1 %collective-permute-start.12 = (bf16[192,4096]{1,0:T(8,128)(2,1)}, bf16[192,4096]{1,0:T(8,128)(2,1)}, u32[]{:S(2)}, u32[]{:S(2)}) collective-permute-start(bf16[192,4096]{1,0:T(8,128)(2,1)} %get-tuple-element.634), channel_id=1, source_target_pairs={{64,0},{128,64},{192,128},{65,1},{129,65},{193,129},{66,2},{130,66... | collective-permute-start | bytes 4718600 | tf_op jit(solution)/shard_map/ppermute | solution.py:14
  184.6 26.2 %collective-permute-done.12 = bf16[192,4096]{1,0:T(8,128)(2,1)} collective-permute-done((bf16[192,4096]{1,0:T(8,128)(2,1)}, bf16[192,4096]{1,0:T(8,128)(2,1)}, u32[]{:S(2)}, u32[]{:S(2)}) %collective-permute-start.12) | collective-permute-done | bytes 1572896 | tf_op jit(solution)/shard_map/ppermute | solution.py:14
  211.0 9.9 %collective-permute-start.14 = (bf16[1,32,256]{2,1,0:T(8,128)(2,1)S(1)}, bf16[1,32,256]{2,1,0:T(8,128)(2,1)S(1)}, u32[]{:S(2)}, u32[]{:S(2)}) collective-permute-start(bf16[1,32,256]{2,1,0:T(8,128)(2,1)S(1)} %get-tuple-element.593), channel_id=1, source_target_pairs={{1,0},{2,1},{3,2},{4,3},{5,4},{6,5},{7,6},{8,7},{9,8},{10,9},{11,1... | collective-permute-start | bytes 49160 | tf_op jit(solution)/shard_map/ppermute | solution.py:25
  223.7 1.9 collective-permute-start.15
  225.7 32.5 %collective-permute-done.15 = bf16[24,32,256]{2,1,0:T(8,128)(2,1)S(1)} collective-permute-done((bf16[24,32,256]{2,1,0:T(8,128)(2,1)S(1)}, bf16[24,32,256]{2,1,0:T(8,128)(2,1)S(1)}, u32[]{:S(2)}, u32[]{:S(2)}) %collective-permute-start.15) | collective-permute-done | bytes 393248 | tf_op jit(solution)/shard_map/ppermute | solution.py:14
  258.2 9.9 %collective-permute-start.17 = (bf16[1,32,256]{2,1,0:T(8,128)(2,1)S(1)}, bf16[1,32,256]{2,1,0:T(8,128)(2,1)S(1)}, u32[]{:S(2)}, u32[]{:S(2)}) collective-permute-start(bf16[1,32,256]{2,1,0:T(8,128)(2,1)S(1)} %get-tuple-element.591), channel_id=1, source_target_pairs={{1,0},{2,1},{3,2},{4,3},{5,4},{6,5},{7,6},{8,7},{9,8},{10,9},{11,1... | collective-permute-start | bytes 49160 | tf_op jit(solution)/shard_map/ppermute | solution.py:25
  269.6 3.4 conditional.25
  275.9 7.2 conditional.26
  276.3 6.0 fusion.84
  283.1 1.9 collective-permute-start.18
  285.0 28.5 %collective-permute-done.18 = bf16[192,4096]{1,0:T(8,128)(2,1)S(1)} collective-permute-done((bf16[192,4096]{1,0:T(8,128)(2,1)S(1)}, bf16[192,4096]{1,0:T(8,128)(2,1)S(1)}, u32[]{:S(2)}, u32[]{:S(2)}) %collective-permute-start.18) | collective-permute-done | bytes 1572896 | tf_op jit(solution)/shard_map/ppermute | solution.py:14
  315.0 9.2 %fusion.110 = f32[4096,1024]{1,0:T(8,128)} fusion(bf16[192,4096]{1,0:T(8,128)(2,1)S(1)} %get-tuple-element.494, bf16[192,1024]{1,0:T(8,128)(2,1)} %get-tuple-element.495), kind=kOutput, calls=%fused_computation.243 | convolution fusion | flops 1610612736 | bytes 18743296 | tf_op jit(solution)/shard_map/dot_general | solution.py:204
  324.2 443.0 %reduce-scatter.2.cloned.1.call-done = f32[64,1024]{1,0:T(8,128)} async-done(((f32[4096,1024]{1,0:T(8,128)}), f32[64,1024]{1,0:T(8,128)}) %reduce-scatter.2.cloned.1.call-update) | async-done | bytes 262160 | tf_op jit(solution)/shard_map/reduce_scatter | solution.py:203
  (128 shorter events, 50.5 us)
Async XLA Ops:
  6.5 760.7 %reduce-scatter.2.cloned.1.call-start = ((), (), s32[]{:S(2)}) async-start(), calls=%async_computation.1 | async-start | bytes 17039360 | tf_op jit(solution)/shard_map/reduce_scatter | solution.py:203
  7.3 11.8 %collective-permute-start = (bf16[1,32,256]{2,1,0:T(8,128)(2,1)S(1)}, bf16[1,32,256]{2,1,0:T(8,128)(2,1)S(1)}, u32[]{:S(2)}, u32[]{:S(2)}) collective-permute-start(bf16[1,32,256]{2,1,0:T(8,128)(2,1)S(1)} %get-tuple-element.600), channel_id=1, source_target_pairs={{0,1},{1,2},{2,3},{3,4},{4,5},{5,6},{6,7},{7,8},{8,9},{9,10},{10,1... | collective-permute-start | bytes 49160 | tf_op jit(solution)/shard_map/ppermute | solution.py:24
  7.3 11.8 %collective-permute-start.1 = (bf16[1,32,256]{2,1,0:T(8,128)(2,1)S(1)}, bf16[1,32,256]{2,1,0:T(8,128)(2,1)S(1)}, u32[]{:S(2)}, u32[]{:S(2)}) collective-permute-start(bf16[1,32,256]{2,1,0:T(8,128)(2,1)S(1)} %get-tuple-element.601), channel_id=1, source_target_pairs={{1,0},{2,1},{3,2},{4,3},{5,4},{6,5},{7,6},{8,7},{9,8},{10,9},{11,1... | collective-permute-start | bytes 49160 | tf_op jit(solution)/shard_map/ppermute | solution.py:25
  20.2 0.8 copy-start.14
  21.4 46.0 %collective-permute-start.2 = (bf16[192,4096]{1,0:T(8,128)(2,1)S(1)}, bf16[192,4096]{1,0:T(8,128)(2,1)S(1)}, u32[]{:S(2)}, u32[]{:S(2)}) collective-permute-start(bf16[192,4096]{1,0:T(8,128)(2,1)S(1)} %get-tuple-element.629), channel_id=1, source_target_pairs={{0,64},{64,128},{128,192},{1,65},{65,129},{129,193},{2,66},{66,130... | collective-permute-start | bytes 4718600 | tf_op jit(solution)/shard_map/ppermute | solution.py:14
  79.7 13.7 %copy-start = (f32[24,32,256]{2,1,0:T(8,128)}, f32[24,32,256]{2,1,0:T(8,128)S(1)}, u32[]{:S(2)}) copy-start(f32[24,32,256]{2,1,0:T(8,128)S(1)} %get-tuple-element.500) | copy-start | bytes 2359300
  81.3 12.0 %collective-permute-start.3 = (bf16[1,32,256]{2,1,0:T(8,128)(2,1)S(1)}, bf16[1,32,256]{2,1,0:T(8,128)(2,1)S(1)}, u32[]{:S(2)}, u32[]{:S(2)}) collective-permute-start(bf16[1,32,256]{2,1,0:T(8,128)(2,1)S(1)} %get-tuple-element.598), channel_id=1, source_target_pairs={{0,1},{1,2},{2,3},{3,4},{4,5},{5,6},{6,7},{7,8},{8,9},{9,10},{10,1... | collective-permute-start | bytes 49160 | tf_op jit(solution)/shard_map/ppermute | solution.py:24
  81.4 12.0 %collective-permute-start.4 = (bf16[1,32,256]{2,1,0:T(8,128)(2,1)S(1)}, bf16[1,32,256]{2,1,0:T(8,128)(2,1)S(1)}, u32[]{:S(2)}, u32[]{:S(2)}) collective-permute-start(bf16[1,32,256]{2,1,0:T(8,128)(2,1)S(1)} %get-tuple-element.599), channel_id=1, source_target_pairs={{1,0},{2,1},{3,2},{4,3},{5,4},{6,5},{7,6},{8,7},{9,8},{10,9},{11,1... | collective-permute-start | bytes 49160 | tf_op jit(solution)/shard_map/ppermute | solution.py:25
  94.3 1.3 copy-start.9
  97.4 9.9 %collective-permute-start.5 = (bf16[24,32,256]{2,1,0:T(8,128)(2,1)}, bf16[24,32,256]{2,1,0:T(8,128)(2,1)S(1)}, u32[]{:S(2)}, u32[]{:S(2)}) collective-permute-start(bf16[24,32,256]{2,1,0:T(8,128)(2,1)} %get-tuple-element.630), channel_id=1, source_target_pairs={{0,64},{64,128},{128,192},{1,65},{65,129},{129,193},{2,66},{66,130... | collective-permute-start | bytes 1179656 | tf_op jit(solution)/shard_map/ppermute | solution.py:14
  107.2 0.8 copy-start.6
  108.3 11.4 %collective-permute-start.6 = (bf16[1,32,256]{2,1,0:T(8,128)(2,1)S(1)}, bf16[1,32,256]{2,1,0:T(8,128)(2,1)S(1)}, u32[]{:S(2)}, u32[]{:S(2)}) collective-permute-start(bf16[1,32,256]{2,1,0:T(8,128)(2,1)S(1)} %get-tuple-element.596), channel_id=1, source_target_pairs={{0,1},{1,2},{2,3},{3,4},{4,5},{5,6},{6,7},{7,8},{8,9},{9,10},{10,1... | collective-permute-start | bytes 49160 | tf_op jit(solution)/shard_map/ppermute | solution.py:24
  108.4 11.3 %collective-permute-start.7 = (bf16[1,32,256]{2,1,0:T(8,128)(2,1)S(1)}, bf16[1,32,256]{2,1,0:T(8,128)(2,1)S(1)}, u32[]{:S(2)}, u32[]{:S(2)}) collective-permute-start(bf16[1,32,256]{2,1,0:T(8,128)(2,1)S(1)} %get-tuple-element.597), channel_id=1, source_target_pairs={{1,0},{2,1},{3,2},{4,3},{5,4},{6,5},{7,6},{8,7},{9,8},{10,9},{11,1... | collective-permute-start | bytes 49160 | tf_op jit(solution)/shard_map/ppermute | solution.py:25
  121.5 14.1 %copy-start.3 = (bf16[24,32,256]{2,1,0:T(8,128)(2,1)S(1)}, bf16[24,32,256]{2,1,0:T(8,128)(2,1)}, u32[]{:S(2)}) copy-start(bf16[24,32,256]{2,1,0:T(8,128)(2,1)} %param.39) | copy-start | bytes 1179652
  121.7 1.2 copy-start.4
  122.8 44.2 %collective-permute-start.8 = (bf16[192,4096]{1,0:T(8,128)(2,1)}, bf16[192,4096]{1,0:T(8,128)(2,1)S(1)}, u32[]{:S(2)}, u32[]{:S(2)}) collective-permute-start(bf16[192,4096]{1,0:T(8,128)(2,1)} %copy-done.4), channel_id=1, source_target_pairs={{0,64},{64,128},{128,192},{1,65},{65,129},{129,193},{2,66},{66,130... | collective-permute-start | bytes 4718600 | tf_op jit(solution)/shard_map/ppermute | solution.py:14
  134.2 19.2 %collective-permute-start.11 = (bf16[24,32,256]{2,1,0:T(8,128)(2,1)}, bf16[24,32,256]{2,1,0:T(8,128)(2,1)}, u32[]{:S(2)}, u32[]{:S(2)}) collective-permute-start(bf16[24,32,256]{2,1,0:T(8,128)(2,1)} %get-tuple-element.628), channel_id=1, source_target_pairs={{0,192},{1,193},{2,194},{3,195},{4,196},{5,197},{6,198},{7,199},{8... | collective-permute-start | bytes 1179656 | tf_op jit(solution)/shard_map/ppermute | solution.py:14
  136.2 14.6 %collective-permute-start.9 = (bf16[1,32,256]{2,1,0:T(8,128)(2,1)}, bf16[1,32,256]{2,1,0:T(8,128)(2,1)}, u32[]{:S(2)}, u32[]{:S(2)}) collective-permute-start(bf16[1,32,256]{2,1,0:T(8,128)(2,1)} %get-tuple-element.594), channel_id=1, source_target_pairs={{0,1},{1,2},{2,3},{3,4},{4,5},{5,6},{6,7},{7,8},{8,9},{9,10},{10,1... | collective-permute-start | bytes 49160 | tf_op jit(solution)/shard_map/ppermute | solution.py:24
  136.2 14.6 %collective-permute-start.10 = (bf16[1,32,256]{2,1,0:T(8,128)(2,1)S(1)}, bf16[1,32,256]{2,1,0:T(8,128)(2,1)}, u32[]{:S(2)}, u32[]{:S(2)}) collective-permute-start(bf16[1,32,256]{2,1,0:T(8,128)(2,1)S(1)} %get-tuple-element.595), channel_id=1, source_target_pairs={{1,0},{2,1},{3,2},{4,3},{5,4},{6,5},{7,6},{8,7},{9,8},{10,9},{11,1... | collective-permute-start | bytes 49160 | tf_op jit(solution)/shard_map/ppermute | solution.py:25
  176.4 34.4 %collective-permute-start.12 = (bf16[192,4096]{1,0:T(8,128)(2,1)}, bf16[192,4096]{1,0:T(8,128)(2,1)}, u32[]{:S(2)}, u32[]{:S(2)}) collective-permute-start(bf16[192,4096]{1,0:T(8,128)(2,1)} %get-tuple-element.634), channel_id=1, source_target_pairs={{64,0},{128,64},{192,128},{65,1},{129,65},{193,129},{66,2},{130,66... | collective-permute-start | bytes 4718600 | tf_op jit(solution)/shard_map/ppermute | solution.py:14
  210.9 11.5 %collective-permute-start.13 = (bf16[1,32,256]{2,1,0:T(8,128)(2,1)S(1)}, bf16[1,32,256]{2,1,0:T(8,128)(2,1)S(1)}, u32[]{:S(2)}, u32[]{:S(2)}) collective-permute-start(bf16[1,32,256]{2,1,0:T(8,128)(2,1)S(1)} %get-tuple-element.592), channel_id=1, source_target_pairs={{0,1},{1,2},{2,3},{3,4},{4,5},{5,6},{6,7},{7,8},{8,9},{9,10},{10,1... | collective-permute-start | bytes 49160 | tf_op jit(solution)/shard_map/ppermute | solution.py:24
  211.0 11.4 %collective-permute-start.14 = (bf16[1,32,256]{2,1,0:T(8,128)(2,1)S(1)}, bf16[1,32,256]{2,1,0:T(8,128)(2,1)S(1)}, u32[]{:S(2)}, u32[]{:S(2)}) collective-permute-start(bf16[1,32,256]{2,1,0:T(8,128)(2,1)S(1)} %get-tuple-element.593), channel_id=1, source_target_pairs={{1,0},{2,1},{3,2},{4,3},{5,4},{6,5},{7,6},{8,7},{9,8},{10,9},{11,1... | collective-permute-start | bytes 49160 | tf_op jit(solution)/shard_map/ppermute | solution.py:25
  222.4 1.0 copy-start.7
  223.7 34.4 %collective-permute-start.15 = (bf16[24,32,256]{2,1,0:T(8,128)(2,1)S(1)}, bf16[24,32,256]{2,1,0:T(8,128)(2,1)S(1)}, u32[]{:S(2)}, u32[]{:S(2)}) collective-permute-start(bf16[24,32,256]{2,1,0:T(8,128)(2,1)S(1)} %fusion.100), channel_id=1, source_target_pairs={{64,0},{128,64},{192,128},{65,1},{129,65},{193,129},{66,2},{130,66... | collective-permute-start | bytes 1179656 | tf_op jit(solution)/shard_map/ppermute | solution.py:14
  258.2 11.3 %collective-permute-start.16 = (bf16[1,32,256]{2,1,0:T(8,128)(2,1)S(1)}, bf16[1,32,256]{2,1,0:T(8,128)(2,1)S(1)}, u32[]{:S(2)}, u32[]{:S(2)}) collective-permute-start(bf16[1,32,256]{2,1,0:T(8,128)(2,1)S(1)} %get-tuple-element.590), channel_id=1, source_target_pairs={{0,1},{1,2},{2,3},{3,4},{4,5},{5,6},{6,7},{7,8},{8,9},{9,10},{10,1... | collective-permute-start | bytes 49160 | tf_op jit(solution)/shard_map/ppermute | solution.py:24
  258.2 11.3 %collective-permute-start.17 = (bf16[1,32,256]{2,1,0:T(8,128)(2,1)S(1)}, bf16[1,32,256]{2,1,0:T(8,128)(2,1)S(1)}, u32[]{:S(2)}, u32[]{:S(2)}) collective-permute-start(bf16[1,32,256]{2,1,0:T(8,128)(2,1)S(1)} %get-tuple-element.591), channel_id=1, source_target_pairs={{1,0},{2,1},{3,2},{4,3},{5,4},{6,5},{7,6},{8,7},{9,8},{10,9},{11,1... | collective-permute-start | bytes 49160 | tf_op jit(solution)/shard_map/ppermute | solution.py:25
  269.6 3.5 copy-start.1
  270.7 1.3 copy-start.13
  275.9 37.7 %copy-start.5 = (bf16[192,1024]{1,0:T(8,128)(2,1)S(1)}, bf16[192,1024]{1,0:T(8,128)(2,1)}, u32[]{:S(2)}) copy-start(bf16[192,1024]{1,0:T(8,128)(2,1)} %reshape.276) | copy-start | bytes 1179652
  283.1 30.4 %collective-permute-start.18 = (bf16[192,4096]{1,0:T(8,128)(2,1)S(1)}, bf16[192,4096]{1,0:T(8,128)(2,1)S(1)}, u32[]{:S(2)}, u32[]{:S(2)}) collective-permute-start(bf16[192,4096]{1,0:T(8,128)(2,1)S(1)} %get-tuple-element.638), channel_id=1, source_target_pairs={{64,0},{128,64},{192,128},{65,1},{129,65},{193,129},{66,2},{130,66... | collective-permute-start | bytes 4718600 | tf_op jit(solution)/shard_map/ppermute | solution.py:14
Sparse Core Ops, SparseCore 0:
  324.3 442.8 reduce-scatter.1
where the time goes:
time: 781 us; the launch traced here: 776 us
  waiting for transfers between devices  601 us (77%)
  starting transfers between devices  90.6 us (12%)
  local copies, waits for them, and re-layouts  27.6 us (4%)
  matrix products  23.8 us (3%)
  other arithmetic  17.3 us (2%)
  between operations  14.2 us (2%)
    reduce_scatter x1, waiting for transfers between devices, on_device(): lax.psum_scatter(jnp.dot(columns.T, patch_side, preferred_element_type=jn...  443 us
    ppermute x7, waiting for transfers between devices, shifted(): return lax.ppermute(value, axis, pairs)  152 us
    ppermute x6, starting transfers between devices, with_halo(): after = lax.ppermute(initial, axis, down)  60.4 us
    ppermute x7, starting transfers between devices, shifted(): return lax.ppermute(value, axis, pairs)  30 us
  transfers between devices with their start and end apart: 20, of which 13 were waited for; matrix products, arithmetic and copies ran while one was open for 1% of the time, Pallas kernels for 0%

commit v1 on v0

v1 whole, which is shorter than its diff:
```python
import math

import jax
import jax.numpy as jnp
from jax import lax
from jax.experimental import pallas as pl
from jax.experimental.pallas import tpu as pltpu
from jax.sharding import PartitionSpec as P

NORM_EPS = 1e-05
BF16 = jnp.bfloat16
F32 = jnp.float32
SIDE = 32
HALF = SIDE // 2
C = 256
N_SEQ = 64
SEQ = "seq"

X1, X3, Y1, Y3, CORE, ZH = (1 << 3, 3 << 3, 1 << 1, 3 << 1, 1, 1 << 5)


def flip(value, mask):
    return lax.ppermute(value, SEQ, [(i, i ^ mask) for i in range(N_SEQ)])


def partner(value):
    return lax.ppermute(value, "section", [(0, 1), (1, 0), (2, 3), (3, 2)])


HOPS = [(1 * N_SEQ + q, 2 * N_SEQ + q) for q in range(N_SEQ)] + [
    (q, 3 * N_SEQ + (q ^ ZH)) for q in range(N_SEQ)
]


def hop_on(value):
    return lax.ppermute(value, ("section", SEQ), HOPS)


def hop_back(value):
    return lax.ppermute(value, ("section", SEQ), [(j, i) for i, j in HOPS])


def dot(left, right):
    return jnp.dot(left, right, preferred_element_type=F32)


def dot_nt(left, right):
    return lax.dot_general(left, right, (((1,), (1,)), ((), ())), preferred_element_type=F32)


def dot_tn(left, right):
    return lax.dot_general(left, right, (((0,), (0,)), ((), ())), preferred_element_type=F32)


def patchify(field):
    pairs = field.reshape(HALF, 2, HALF, 2 * C)
    return jnp.concatenate([pairs[:, 0], pairs[:, 1]], axis=-1).reshape(HALF * HALF, 4 * C)


def unpatchify(tokens):
    pairs = tokens.reshape(HALF, HALF, 4 * C)
    return jnp.stack([pairs[..., : 2 * C], pairs[..., 2 * C :]], axis=1).reshape(SIDE, HALF, 2 * C)


def silu_slope(value):
    sigma = jax.nn.sigmoid(value)
    return sigma * (1.0 + value * (1.0 - sigma))


CHUNKS = 8
VMEM = pl.BlockSpec(memory_space=pltpu.VMEM)
SMEM = pl.BlockSpec(memory_space=pltpu.SMEM)
ANY = pl.BlockSpec(memory_space=pl.ANY)


def conv_in_kernel(field, kernel_ref, left_ref, right_ref, turned=False):
    even, odd = field[..., :C], field[..., C:]
    column = lax.broadcasted_iota(jnp.int32, (SIDE, HALF, C), 1)
    before = jnp.where(column == 0, 0.0, pltpu.roll(odd, 1, 1))
    after = jnp.where(column == HALF - 1, 0.0, pltpu.roll(even, HALF - 1, 1))
    middle = field.astype(BF16)
    left_ref[1 : SIDE + 1, :, C:] = middle
    left_ref[1 : SIDE + 1, :, :C] = before.astype(BF16)
    right_ref[1 : SIDE + 1, :, : 2 * C] = middle
    right_ref[1 : SIDE + 1, :, 2 * C :] = after.astype(BF16)
    out = []
    for ref in (left_ref, right_ref):
        edge = jnp.zeros((HALF, 3 * C), BF16)
        ref[0] = edge
        ref[SIDE + 1] = edge
        total = None
        for row in range(3):
            taps = ref[row : row + SIDE].reshape(SIDE * HALF, 3 * C)
            if turned:
                for column in range(3):
                    tap = (2 - row) * 3 + 2 - column
                    weight = kernel_ref[tap * C : (tap + 1) * C]
                    term = dot_nt(taps[:, column * C : (column + 1) * C], weight)
                    total = term if total is None else total + term
            else:
                term = dot(taps, kernel_ref[row * 3 * C : (row + 1) * 3 * C])
                total = term if total is None else total + term
        out.append(total.reshape(SIDE, HALF, C))
    return jnp.concatenate(out, axis=-1)


def choose(to_ref, mine, own_ref, other_ref):
    @pl.when(mine)
    def _():
        to_ref[...] = own_ref[...]

    @pl.when(jnp.logical_not(mine))
    def _():
        to_ref[...] = other_ref[...]


def rounded(value):
    return value.astype(BF16).astype(F32)


def silu(value):
    return value * jax.nn.sigmoid(value)


class Weights:
    def __init__(self, index_ref, own_ref, near_ref, far_ref, parity):
        self.args = (index_ref, own_ref, near_ref, far_ref, parity)
        self.rows = own_ref.shape[0] // CHUNKS
        self.share = own_ref.shape[0] // N_SEQ

    def own_chunk(self, chunk):
        index_ref, own_ref = self.args[:2]
        per = N_SEQ // CHUNKS
        starts = [
            pl.multiple_of(index_ref[chunk * per + i] * self.share, self.share) for i in range(per)
        ]
        return jnp.concatenate([own_ref[pl.ds(start, self.share)] for start in starts], axis=0)

    def sweep(self, slot, step):
        _, _, near_ref, far_ref, parity = self.args

        @pl.when(parity == slot)
        def _():
            @pl.loop(0, CHUNKS)
            def _(chunk):
                step(chunk, self.own_chunk(chunk))

        @pl.when(parity != slot)
        def _():
            sweep_other(near_ref, far_ref, step)


def sweep_other(near_ref, far_ref, step):
    half = CHUNKS // 2
    rows = near_ref.shape[0] // half
    for first, ref in ((0, near_ref), (half, far_ref)):

        @pl.loop(0, half)
        def _(i, first=first, ref=ref):
            step(first + i, ref[pl.ds(pl.multiple_of(i * rows, rows), rows)])


def lanes(chunk, count):
    return pl.ds(pl.multiple_of(chunk * count, count), count)


TAPS = [pltpu.VMEM((SIDE + 2, HALF, 3 * C), BF16)] * 2
TOKENS = HALF * HALF
KERNEL = [pltpu.VMEM((9 * C, C), BF16)]
PARAMS = pltpu.CompilerParams(vmem_limit_bytes=40 * 1024 * 1024)


def call(body, outs, args):
    return pl.pallas_call(
        body,
        out_shape=[jax.ShapeDtypeStruct(shape, kind) for shape, kind in outs],
        in_specs=[VMEM] * len(args),
        out_specs=[VMEM] * len(outs),
        compiler_params=PARAMS,
    )(*args)


def run_start(section, phase, rows, late, near, kernels):
    def body(
        section_ref, phase_ref, rows_ref, late_ref, near_ref, own_kernel_ref, other_kernel_ref,
        skip_ref, start_ref, image_ref, left_ref, right_ref, kernel_ref,
    ):
        where, kind = section_ref[0], phase_ref[0]
        choose(kernel_ref, (where == 0) | (where == 3), own_kernel_ref, other_kernel_ref)

        @pl.when(kind == 0)
        def _():
            image_ref[:16] = late_ref[...]
            image_ref[16:] = rows_ref[:16]

        @pl.when(kind == 1)
        def _():
            image_ref[:8] = near_ref[...]
            image_ref[8:] = rows_ref[...]

        @pl.when(kind == 2)
        def _():
            image_ref[:24] = rows_ref[...]
            image_ref[24:] = near_ref[...]

        @pl.when(kind == 3)
        def _():
            image_ref[...] = jnp.zeros_like(image_ref)

        @pl.when(where < 2)
        def _():
            field = conv_in_kernel(image_ref[...], kernel_ref, left_ref, right_ref)
            skip_ref[...] = field.astype(BF16)

        @pl.when(where >= 2)
        def _():
            field = conv_in_kernel(image_ref[...], kernel_ref, left_ref, right_ref, turned=True)
            start_ref[...] = field

    shape = (SIDE, HALF, 2 * C)
    return pl.pallas_call(
        body,
        out_shape=[jax.ShapeDtypeStruct(shape, BF16), jax.ShapeDtypeStruct(shape, F32)],
        in_specs=[SMEM, SMEM] + [VMEM] * 5,
        out_specs=[VMEM] * 2,
        scratch_shapes=[pltpu.VMEM(shape, F32)] + TAPS + KERNEL,
        compiler_params=PARAMS,
        name="start",
    )(section, phase, rows, late, near, *kernels)


def run_piece(blocks, weight):
    share, depth = weight.shape[0] // N_SEQ, weight.shape[1]

    def body(index_ref, weight_ref, out_ref):
        out_ref[...] = weight_ref[...]

    return pl.pallas_call(
        body,
        grid_spec=pltpu.PrefetchScalarGridSpec(
            num_scalar_prefetch=1,
            grid=(2,),
            in_specs=[pl.BlockSpec((share, depth), lambda i, index: (index[i], 0))],
            out_specs=pl.BlockSpec((share, depth), lambda i, index: (i, 0)),
        ),
        out_shape=jax.ShapeDtypeStruct((2 * share, depth), weight.dtype),
    )(blocks, weight)


def gather_partner(piece):
    rows, depth = piece.shape
    half, part = depth // 2, depth // 4

    def split(piece_ref, first_ref, second_ref):
        first_ref[...] = piece_ref[:, :half]
        second_ref[...] = piece_ref[:, half:]

    shape = (rows, half)
    first, second = call(split, [(shape, BF16)] * 2, (piece,))
    got = [flip(first, m) for m in (X1, X1 ^ X3, X3)] + [flip(second, m) for m in (Y1, Y1 ^ Y3, Y3)]

    def stack(*refs):
        for side in range(2):
            for far in range(4):
                source = refs[side] if far == 0 else refs[2 + 3 * side + far - 1]
                refs[8 + side][far * rows : (far + 1) * rows] = source[...]

    shape = (4 * rows, half)
    wide = call(stack, [(shape, BF16)] * 2, (first, second, *got))
    rings = ((Y1, Y3), (X1, X3))
    near = [flip(value, ring[0]) for value, ring in zip(wide, rings)]
    far = [flip(value, ring[1]) for value, ring in zip(wide, rings)]

    def cut(*refs):
        for side in range(2):
            refs[4 + 2 * side][...] = refs[side][:, :part]
            refs[5 + 2 * side][...] = refs[2 + side][:, part:]

    shape = (4 * rows, part)
    parts = call(cut, [(shape, BF16)] * 4, (*far, *near))
    low = [flip(parts[2 * side], ring[0]) for side, ring in enumerate(rings)]
    high = [flip(parts[2 * side + 1], ring[1]) for side, ring in enumerate(rings)]

    def join(*refs):
        out_ref = refs[10]
        for side in range(2):
            base = side * half
            mine, one, three = refs[side], refs[2 + side], refs[4 + side]
            for outer in range(4):
                sources = {0: [mine], 1: [one], 3: [three], 2: [refs[6 + side], refs[8 + side]]}[outer]
                for j, source in enumerate(sources):
                    count = source.shape[1]
                    at = slice(base + j * count, base + (j + 1) * count)
                    for inner in range(4):
                        block = source[inner * rows : (inner + 1) * rows]
                        x, y = (inner, outer) if side == 0 else (outer, inner)
                        start = (4 * x + y) * rows
                        out_ref[start : start + rows, at] = block

    args = (*wide, *near, *far, *low, *high)
    return call(join, [((16 * rows, depth), BF16)], args)[0]


def run_forward(section, blocks, skip, own, near, far, codes, kernels):
    width, depth = own.shape
    cols = width // CHUNKS

    def body(
        section_ref, index_ref, skip_ref, own_ref, near_ref, far_ref, one_ref, two_ref, cos_ref,
        sin_ref, own_kernel_ref, other_kernel_ref, tokens_ref, act_ref, lift_ref, field_ref, sum_ref,
        left_ref, right_ref, kernel_ref,
    ):
        parity = section_ref[0] % 2

        @pl.when(section_ref[0] < 2)
        def _():
            weights = Weights(index_ref, own_ref, near_ref, far_ref, parity)
            choose(kernel_ref, parity == 1, own_kernel_ref, other_kernel_ref)
            patch = patchify(skip_ref[...])
            sum_ref[...] = jnp.zeros_like(sum_ref)

            def embed(chunk, rows):
                at = lanes(chunk, cols)
                code = one_ref[:, at][:, None] * cos_ref[:, at][None]
                code += two_ref[:, at][:, None] * sin_ref[:, at][None]
                value = dot_nt(patch, rows) + code.reshape(TOKENS, cols)
                value = value.astype(BF16)
                tokens_ref[:, at] = value
                value = value.astype(F32)
                sum_ref[...] += jnp.sum(value * value, axis=-1, keepdims=True)

            weights.sweep(0, embed)
            scale = lax.rsqrt(sum_ref[...] * (1.0 / width) + NORM_EPS)
            lift_ref[...] = jnp.zeros_like(lift_ref)

            def raise_up(chunk, rows):
                at = lanes(chunk, cols)
                active = silu(tokens_ref[:, at].astype(F32) * scale).astype(BF16)
                act_ref[:, at] = active
                lift_ref[...] += dot(active, rows)

            weights.sweep(1, raise_up)

            field = unpatchify(rounded(silu(lift_ref[...])))
            field_ref[...] = conv_in_kernel(field, kernel_ref, left_ref, right_ref).astype(BF16)

    return pl.pallas_call(
        body,
        out_shape=[
            jax.ShapeDtypeStruct((TOKENS, width), BF16),
            jax.ShapeDtypeStruct((TOKENS, width), BF16),
            jax.ShapeDtypeStruct((TOKENS, depth), F32),
            jax.ShapeDtypeStruct((SIDE, HALF, 2 * C), BF16),
        ],
        in_specs=[SMEM, SMEM] + [VMEM] * 10,
        out_specs=[VMEM] * 4,
        scratch_shapes=[pltpu.VMEM((TOKENS, 1), F32)] + TAPS + KERNEL,
        compiler_params=PARAMS,
        name="forward_first_pair",
    )(section, blocks, skip, own, near, far, *codes, *kernels)


def run_second_pair(section, blocks, second, skip, start, own, near, far, kernels):
    width, depth = own.shape
    cols = width // CHUNKS

    def body(
        section_ref, index_ref, second_ref, skip_ref, start_ref, own_ref, near_ref, far_ref,
        own_kernel_ref, other_kernel_ref, back_ref, side_ref, patch_ref, sum_ref, left_ref,
        right_ref, kernel_ref, tokens_ref, inner_ref, lift_ref,
    ):
        parity = section_ref[0] % 2

        @pl.when(section_ref[0] >= 2)
        def _():
            weights = Weights(index_ref, own_ref, near_ref, far_ref, parity)
            choose(kernel_ref, parity == 0, own_kernel_ref, other_kernel_ref)
            field = rounded(silu(second_ref[...].astype(F32)))
            field = conv_in_kernel(field, kernel_ref, left_ref, right_ref).astype(BF16)
            patch_ref[...] = patchify(field)
            sum_ref[...] = jnp.zeros_like(sum_ref)

            def embed(chunk, rows):
                value = dot_nt(patch_ref[...], rows).astype(BF16)
                tokens_ref[:, lanes(chunk, cols)] = value
                value = value.astype(F32)
                sum_ref[...] += jnp.sum(value * value, axis=-1, keepdims=True)

            weights.sweep(0, embed)
            scale = lax.rsqrt(sum_ref[...] * (1.0 / width) + NORM_EPS)
            lift_ref[...] = patchify(skip_ref[...]).astype(F32)

            def raise_up(chunk, rows):
                at = lanes(chunk, cols)
                active = silu(tokens_ref[:, at].astype(F32) * scale).astype(BF16)
                side_ref[:, at] = active
                lift_ref[...] += dot(active, rows)

            weights.sweep(1, raise_up)
            last_patch = (patchify(start_ref[...]) * silu_slope(lift_ref[...])).astype(BF16)

            @pl.when(parity == 1)
            def _():
                patch_ref[...] = last_patch

            sum_ref[...] = jnp.zeros_like(sum_ref)

            def descend(chunk, rows):
                at = lanes(chunk, cols)
                normal = tokens_ref[:, at].astype(F32) * scale
                inner = dot_nt(last_patch, rows) * silu_slope(normal)
                inner_ref[:, at] = inner
                sum_ref[...] += jnp.sum(inner * normal, axis=-1, keepdims=True)

            weights.sweep(1, descend)
            mean = sum_ref[...] * (1.0 / width)
            lift_ref[...] = jnp.zeros_like(lift_ref)

            def lower(chunk, rows):
                at = lanes(chunk, cols)
                normal = tokens_ref[:, at].astype(F32) * scale
                back = (scale * (inner_ref[:, at] - normal * mean)).astype(BF16)

                @pl.when(parity == 0)
                def _():
                    side_ref[:, at] = back

                lift_ref[...] += dot(back, rows)

            weights.sweep(0, lower)
            field = unpatchify(rounded(lift_ref[...]))
            field = conv_in_kernel(field, kernel_ref, left_ref, right_ref, turned=True)
            back_ref[...] = (field * silu_slope(second_ref[...].astype(F32))).astype(BF16)

    return pl.pallas_call(
        body,
        out_shape=[
            jax.ShapeDtypeStruct((SIDE, HALF, 2 * C), BF16),
            jax.ShapeDtypeStruct((TOKENS, width), BF16),
            jax.ShapeDtypeStruct((TOKENS, depth), BF16),
        ],
        in_specs=[SMEM, SMEM] + [VMEM] * 8,
        out_specs=[VMEM] * 3,
        scratch_shapes=[pltpu.VMEM((TOKENS, 1), F32)]
        + TAPS
        + KERNEL
        + [
            pltpu.VMEM((TOKENS, width), BF16),
            pltpu.VMEM((TOKENS, width), F32),
            pltpu.VMEM((TOKENS, depth), F32),
        ],
        compiler_params=PARAMS,
        name="second_pair",
    )(section, blocks, second, skip, start, own, near, far, *kernels)


def run_back(section, given, skip, lift, tokens, prior, patch, near, far, kernels):
    width, depth = tokens.shape[1], lift.shape[1]
    cols = width // CHUNKS

    def body(
        section_ref, given_ref, skip_ref, lift_ref, tokens_ref, prior_ref, known_ref, near_ref,
        far_ref, own_kernel_ref, other_kernel_ref, keep_ref, send_ref, patch_ref, sum_ref, left_ref,
        right_ref, kernel_ref, inner_ref,
    ):
        where = section_ref[0]

        @pl.when(where >= 1)
        def _():
            keep_ref[...] = prior_ref[:, : width // 2]
            send_ref[...] = prior_ref[:, width // 2 :]

        @pl.when(where >= 2)
        def _():
            patch_ref[...] = known_ref[...]

        @pl.when(where < 2)
        def _():
            choose(kernel_ref, where == 1, own_kernel_ref, other_kernel_ref)
            field = given_ref[...].astype(F32)
            field = conv_in_kernel(field, kernel_ref, left_ref, right_ref, turned=True)
            patch_ref[...] = (patchify(field) * silu_slope(lift_ref[...])).astype(BF16)

        @pl.when(where == 0)
        def _():
            sum_ref[...] = jnp.zeros_like(sum_ref)

            @pl.loop(0, CHUNKS)
            def _(chunk):
                value = tokens_ref[:, lanes(chunk, cols)].astype(F32)
                sum_ref[...] += jnp.sum(value * value, axis=-1, keepdims=True)

            scale = lax.rsqrt(sum_ref[...] * (1.0 / width) + NORM_EPS)
            sum_ref[...] = jnp.zeros_like(sum_ref)

            def descend(chunk, rows):
                at = lanes(chunk, cols)
                normal = tokens_ref[:, at].astype(F32) * scale
                inner = dot_nt(patch_ref[...], rows) * silu_slope(normal)
                inner_ref[:, at] = inner
                sum_ref[...] += jnp.sum(inner * normal, axis=-1, keepdims=True)

            sweep_other(near_ref, far_ref, descend)
            mean = sum_ref[...] * (1.0 / width)

            for first, ref in ((0, keep_ref), (CHUNKS // 2, send_ref)):

                @pl.loop(0, CHUNKS // 2)
                def _(i, first=first, ref=ref):
                    at = lanes(first + i, cols)
                    normal = tokens_ref[:, at].astype(F32) * scale
                    back = scale * (inner_ref[:, at] - normal * mean)
                    ref[:, lanes(i, cols)] = back.astype(BF16)

            patch_ref[...] = patchify(skip_ref[...])

    return pl.pallas_call(
        body,
        out_shape=[
            jax.ShapeDtypeStruct((TOKENS, width // 2), BF16),
            jax.ShapeDtypeStruct((TOKENS, width // 2), BF16),
            jax.ShapeDtypeStruct((TOKENS, depth), BF16),
        ],
        in_specs=[SMEM] + [VMEM] * 10,
        out_specs=[VMEM] * 3,
        scratch_shapes=[pltpu.VMEM((TOKENS, 1), F32)] + TAPS + KERNEL + [pltpu.VMEM((TOKENS, width), F32)],
        compiler_params=PARAMS,
        name="back_first_pair",
    )(section, given, skip, lift, tokens, prior, patch, near, far, *kernels)


SENT = {"a": (1, 2), "b": (3, 2)}
KEPT = {"a": (0, 3), "b": (0, 1)}


def run_partial(keep, recv, patch, patch_recv):
    half, depth = keep.shape[1], patch.shape[1]
    part, block = depth // 4, half // 16

    def body(keep_ref, recv_ref, patch_ref, other_ref, *out_refs):
        tokens = jnp.concatenate([keep_ref[...], recv_ref[...]], axis=0)
        patches = jnp.concatenate([patch_ref[...], other_ref[...]], axis=0)
        for column in range(4):
            name = "ab"[column % 2]
            sent_ref, kept_ref = out_refs[column], out_refs[4 + column]
            right = patches[:, column * part : (column + 1) * part]
            for i in range(2):
                for ref, far in ((sent_ref, SENT[name][i]), (kept_ref, KEPT[name][i])):
                    if column < 2:
                        left = tokens[:, far * 4 * block : (far + 1) * 4 * block]
                    else:
                        left = jnp.concatenate(
                            [tokens[:, (4 * j + far) * block :][:, :block] for j in range(4)], axis=1
                        )
                    ref[i] = dot_tn(left, right).astype(ref.dtype)

    shape = (2, 4 * block, part)
    outs = call(body, [(shape, BF16)] * 4 + [(shape, F32)] * 4, (keep, recv, patch, patch_recv))
    return outs[:4], outs[4:]


FIRST_RINGS = ((X1, X3), (X3, X1), (Y1, Y3), (Y3, Y1))


def run_sum(partial):
    sent, kept = partial
    got = [flip(value, ring[0]) for value, ring in zip(sent, FIRST_RINGS)]
    rows, part = kept[0].shape[1:]
    block = rows // 4

    def add_once(*refs):
        kept_refs, got_refs, sent_refs, out_refs = refs[:4], refs[4:8], refs[8:12], refs[12:]
        for kept_ref, got_ref, sent_ref, out_ref in zip(kept_refs, got_refs, sent_refs, out_refs):
            total = kept_ref[...] + got_ref[...].astype(F32)
            out_ref[...] = total[0]
            sent_ref[...] = total[1].astype(BF16)

    shape = (rows, part)
    outs = call(add_once, [(shape, BF16)] * 4 + [(shape, F32)] * 4, (*kept, *got))
    got = [flip(value, ring[1]) for value, ring in zip(outs[:4], FIRST_RINGS)]

    def add_twice(*refs):
        kept_refs, got_refs, out_refs = refs[:4], refs[4:8], refs[8:]
        for half in range(2):
            a, b = 2 * half, 2 * half + 1
            total = [kept_refs[i][...] + got_refs[i][...].astype(F32) for i in (a, b)]
            total = jnp.concatenate(total, axis=1)
            for far in range(4):
                ref = out_refs[4 * half + far]
                ref[...] = total[far * block : (far + 1) * block].astype(ref.dtype)

    shape = (block, 2 * part)
    kinds = [F32, BF16, BF16, BF16] * 2
    outs = call(add_twice, [(shape, kind) for kind in kinds], (*outs[4:], *got))
    got = [flip(v, m) for v, m in zip(outs[1:4], (Y1, Y1 ^ Y3, Y3))]
    got += [flip(v, m) for v, m in zip(outs[5:8], (X1, X1 ^ X3, X3))]

    def add_last(*refs):
        for half in range(2):
            total = refs[half][...]
            for ref in refs[2 + 3 * half : 5 + 3 * half]:
                total += ref[...].astype(F32)
            at = slice(half * 2 * part, (half + 1) * 2 * part)
            refs[8][:, at] = total[: block // 2]
            refs[9][:, at] = total[block // 2 :].astype(BF16)

    shape = (block // 2, 4 * part)
    mine, away = call(add_last, [(shape, F32), (shape, BF16)], (outs[0], outs[4], *got))
    return mine + flip(away, ZH).astype(F32)


def on_device(features, conv_kernels, patch_weights, positions, out_cotangent):
    weight = patch_weights[0]
    width, depth = weight.shape
    kernel = conv_kernels[0].reshape(9 * C, C)
    section = lax.axis_index("section")
    place = lax.axis_index(SEQ)
    first_pair = section < 2

    order = jnp.arange(N_SEQ, dtype=jnp.int32)
    away = ((order & 1) << 5) | (((order >> 3) & 3) << 3) | (((order >> 1) & 3) << 1) | (order >> 5)
    blocks = away ^ place

    here, phase = section.reshape(1), (place % 4).reshape(1)
    near = gather_partner(partner(run_piece(blocks, weight)))
    far = flip(near, CORE)
    kernels = (kernel, partner(kernel))

    across = lax.ppermute(
        out_cotangent, ("section", SEQ), [(q, 3 * N_SEQ + (q ^ ZH)) for q in range(N_SEQ)]
    )
    rows = jnp.where(first_pair, features, jnp.where(section == 3, across, out_cotangent))
    rows = rows.astype(F32).reshape(rows.shape[0], HALF, 2 * C)
    late = lax.ppermute(rows[8:], SEQ, [(4 * k + 3, (4 * k + 4) % N_SEQ) for k in range(N_SEQ // 4)])
    some = jnp.where(phase[0] == 0, rows[16:], rows[:8])
    pairs = [(4 * k, 4 * k + 1) for k in range(N_SEQ // 4)]
    pairs += [(4 * k + 3, 4 * k + 2) for k in range(N_SEQ // 4)]
    beside = lax.ppermute(some, SEQ, pairs)
    skip_field, start = run_start(here, phase, rows, late, beside, kernels)
    skip_recv = hop_on(skip_field)

    image_id = jnp.minimum(3 * (place // 4) + place % 4, positions.shape[0] - 1)
    begin = positions[image_id]
    half = width // 2
    feature = (blocks[:, None] * (width // N_SEQ) + jnp.arange(width // N_SEQ)[None, :]).reshape(-1)
    rates = jnp.exp((feature % half).astype(F32) * (-math.log(10000.0) / half))
    is_sin = (feature < half)[None, :]
    steps = jnp.arange(HALF, dtype=jnp.int32)
    row_angle = (begin + HALF * steps).astype(F32)[:, None] * rates[None, :]
    col_angle = steps.astype(F32)[:, None] * rates[None, :]
    row_sin, row_cos = jnp.sin(row_angle), jnp.cos(row_angle)
    row_one = jnp.where(is_sin, row_sin, row_cos)
    row_two = jnp.where(is_sin, row_cos, -row_sin)
    col_cos, col_sin = jnp.cos(col_angle), jnp.sin(col_angle)

    codes = (row_one, row_two, col_cos, col_sin)
    tokens, active, first_lift, second_field = run_forward(
        here, blocks, skip_field, weight, near, far, codes, kernels
    )
    second_back, side, patch = run_second_pair(
        here, blocks, hop_on(second_field), skip_recv, start, weight, near, far, kernels
    )
    prior = jnp.where(first_pair, active, side)
    keep, send, patch = run_back(
        here, hop_back(second_back), skip_field, first_lift, tokens, prior, patch, near, far,
        kernels,
    )

    summed = run_sum(run_partial(keep, flip(send, CORE), patch, flip(patch, CORE)))
    tokens_in_all = positions.shape[0] * HALF * HALF
    return (summed * (1.0 / math.sqrt(tokens_in_all)))[None]


def solution(mesh):
    in_specs = (
        P("seq", None, None),
        P("section", None, None, None, None),
        P("section", None, None),
        P(),
        P("seq", None, None),
    )
    out_specs = P("section", "seq", None)
    return jax.shard_map(
        on_device, mesh=mesh, in_specs=in_specs, out_specs=out_specs, check_vma=False
    )
```

time: 781 us -> 259 us (0.33)
  the two profiles are of different devices: /device:TPU:32 before, /device:TPU:6 now
where the time goes in v1:
time: 259 us; the launch traced here: 256 us
  waiting for transfers between devices  120 us (46%)
  starting transfers between devices  67.5 us (26%)
  Pallas kernels  54.3 us (21%)
  other arithmetic  7.53 us (3%)
  local copies, waits for them, and re-layouts  6.04 us (2%)
    ppermute x32, waiting for transfers between devices, flip(): return lax.ppermute(value, SEQ, [(i, i ^ mask) for i in range(N_SEQ)])  58.3 us
    ppermute x32, starting transfers between devices, flip(): return lax.ppermute(value, SEQ, [(i, i ^ mask) for i in range(N_SEQ)])  46.8 us
    ppermute x1, waiting for transfers between devices, hop_back(): return lax.ppermute(value, ('section', SEQ), [(j, i) for i, j in HOPS])  34.8 us
    pallas_call x1, Pallas kernels, run_forward(): pl.pallas_call(body, out_shape=[jax.ShapeDtypeStruct((TOKENS, width), BF1...  16.6 us
    pallas_call x1, Pallas kernels, run_second_pair(): pl.pallas_call(body, out_shape=[jax.ShapeDtypeStruct((SIDE, HALF, 2 * C),...  14.7 us
    pallas_call x1, Pallas kernels, run_back(): pl.pallas_call(body, out_shape=[jax.ShapeDtypeStruct((TOKENS, width // 2)...  12.4 us
    ppermute x2, waiting for transfers between devices, hop_on(): return lax.ppermute(value, ('section', SEQ), HOPS)  8.28 us
    ppermute x1, starting transfers between devices, on_device(): lax.ppermute(out_cotangent, ('section', SEQ), [(q, 3 * N_SEQ + (q ^ ZH))...  7.79 us
  transfers between devices with their start and end apart: 40, of which 29 were waited for; matrix products, arithmetic and copies ran while one was open for 4% of the time, Pallas kernels for 8%

profile of v1, /device:TPU:6, one launch (start us, length us, event | category | flops | bytes accessed | tf_op | source)
XLA Modules:
  0.0 255.8 jit_solution(11835302791132910840)
XLA Ops:
  0.6 2.3 shard_map.55
  4.8 6.5 %collective-permute-done.4.piece_ref = bf16[128,1024]{1,0:T(8,128)(2,1)S(1)} collective-permute-done((bf16[128,1024]{1,0:T(8,128)(2,1)}, bf16[128,1024]{1,0:T(8,128)(2,1)S(1)}, u32[]{:S(2)}, u32[]{:S(2)}) %collective-permute-start.4) | collective-permute-done | bytes 262176 | tf_op jit(solution)/shard_map/ppermute | solution.py:27
  11.9 2.4 collective-permute-start.6
  15.5 3.0 %collective-permute-start.10 = (bf16[128,512]{1,0:T(8,128)(2,1)S(1)}, bf16[128,512]{1,0:T(8,128)(2,1)S(1)}, u32[]{:S(2)}, u32[]{:S(2)}) collective-permute-start(bf16[128,512]{1,0:T(8,128)(2,1)S(1)} %get-tuple-element.53.refs_1_), channel_id=1, source_target_pairs={{0,6},{1,7},{2,4},{3,5},{4,2},{5,3},{6,0},{7,1},{8,14},{9,15},{10,... | collective-permute-start | bytes 393224 | tf_op jit(solution)/shard_map/ppermute | solution.py:23
  23.1 2.4 collective-permute-done.9.refs_6_
  25.6 2.9 %collective-permute-start.13 = (bf16[512,512]{1,0:T(8,128)(2,1)S(1)}, bf16[512,512]{1,0:T(8,128)(2,1)S(1)}, u32[]{:S(2)}, u32[]{:S(2)}) collective-permute-start(bf16[512,512]{1,0:T(8,128)(2,1)S(1)} %get-tuple-element.54.refs_0_), channel_id=1, source_target_pairs={{0,6},{1,7},{2,4},{3,5},{4,2},{5,3},{6,0},{7,1},{8,14},{9,15},{10,... | collective-permute-start | bytes 1572872 | tf_op jit(solution)/shard_map/ppermute | solution.py:23
  28.7 11.0 %collective-permute-done.13.refs_0_.refs_4_ = bf16[512,512]{1,0:T(8,128)(2,1)S(1)} collective-permute-done((bf16[512,512]{1,0:T(8,128)(2,1)S(1)}, bf16[512,512]{1,0:T(8,128)(2,1)S(1)}, u32[]{:S(2)}, u32[]{:S(2)}) %collective-permute-start.13) | collective-permute-done | bytes 524320 | tf_op jit(solution)/shard_map/ppermute | solution.py:23
  46.7 2.2 collective-permute-done.15.refs_6_
  52.2 2.4 shard_map.59.near_ref
  54.6 7.8 %collective-permute-start = (bf16[24,32,256]{2,1,0:T(8,128)(2,1)S(1)}, bf16[24,32,256]{2,1,0:T(8,128)(2,1)S(1)}, u32[]{:S(2)}, u32[]{:S(2)}) collective-permute-start(bf16[24,32,256]{2,1,0:T(8,128)(2,1)S(1)} %copy-done.7), channel_id=1, source_target_pairs={{0,224},{1,225},{2,226},{3,227},{4,228},{5,229},{6,230},{7,231},{8... | collective-permute-start | bytes 1179656 | tf_op jit(solution)/shard_map/ppermute | solution.py:629
  67.7 3.7 %collective-permute-done = bf16[24,32,256]{2,1,0:T(8,128)(2,1)S(1)} collective-permute-done((bf16[24,32,256]{2,1,0:T(8,128)(2,1)S(1)}, bf16[24,32,256]{2,1,0:T(8,128)(2,1)S(1)}, u32[]{:S(2)}, u32[]{:S(2)}) %collective-permute-start) | collective-permute-done | bytes 393248 | tf_op jit(solution)/shard_map/ppermute | solution.py:629
  73.2 2.3 collective-permute-start.2
  78.1 2.8 %multiply_sine_fusion = (f32[16,4096]{1,0:T(8,128)S(1)}, f32[16,4096]{1,0:T(8,128)}, f32[16,4096]{1,0:T(8,128)}, f32[16,4096]{1,0:T(8,128)}) fusion(f32[16]{0:T(128)S(1)} %copy-done.10, f32[4096]{0:T(1024)S(1)} %copy-done.8, f32[16]{0:T(128)S(1)} %copy-done.11, pred[4096]{0:T(1024)(128)(4,1)S(1)} %copy-done.9), kind=kLoop, calls=%fused_computation.2 | loop fusion | flops 327680 | bytes 1069184 | tf_op jit(solution)/shard_map/sin | solution.py:654
  82.2 7.2 %collective-permute-done.1.late_ref = f32[16,16,512]{2,1,0:T(8,128)} collective-permute-done((f32[16,16,512]{2,1,0:T(8,128)}, f32[16,16,512]{2,1,0:T(8,128)}, u32[]{:S(2)}, u32[]{:S(2)}) %collective-permute-start.1) | collective-permute-done | bytes 524320 | tf_op jit(solution)/shard_map/ppermute | solution.py:634
  90.6 2.7 %start.1 = (bf16[32,16,512]{2,1,0:T(8,128)(2,1)S(1)}, f32[32,16,512]{2,1,0:T(8,128)S(1)}) custom-call(s32[1]{0:T(128)} %bitcast.section_ref, s32[1]{0:T(128)} %bitcast.1.phase_ref, f32[24,16,512]{2,1,0:T(8,128)S(1)} %reshape.81.rows_ref, f32[16,16,512]{2,1,0:T(8,128)} %collective-permute-done.1.late_ref, f32[8,16,512]{2,1,0:T(8,128)} %collective-permute-done.2.near_ref, ...), custom_call_target="tpu_custom_call" | custom-call | tf_op jit(solution)/shard_map/start/pallas_call | solution.py:221
  93.3 4.4 %collective-permute-start.21 = (bf16[32,16,512]{2,1,0:T(8,128)(2,1)S(1)}, bf16[32,16,512]{2,1,0:T(8,128)(2,1)S(1)}, u32[]{:S(2)}, u32[]{:S(2)}) collective-permute-start(bf16[32,16,512]{2,1,0:T(8,128)(2,1)S(1)} %get-tuple-element.51.skip_ref), channel_id=1, source_target_pairs={{64,128},{65,129},{66,130},{67,131},{68,132},{69,133},{70,134},{71... | collective-permute-start | bytes 1572872 | tf_op jit(solution)/shard_map/ppermute | solution.py:36
  97.8 16.6 %forward_first_pair.1 = (bf16[256,4096]{1,0:T(8,128)(2,1)S(1)}, bf16[256,4096]{1,0:T(8,128)(2,1)S(1)}, f32[256,1024]{1,0:T(8,128)S(1)}, bf16[32,16,512]{2,1,0:T(8,128)(2,1)S(1)}) custom-call(s32[1]{0:T(128)} %bitcast.section_ref, s32[64]{0:T(128)S(1)} %copy-done.4, bf16[32,16,512]{2,1,0:T(8,128)(2,1)S(1)} %get-tuple-element.51.skip_ref, ...), custom_call_target="tpu_custom_call" | custom-call | tf_op jit(solution)/shard_map/forward_first_pair/pallas_call | solution.py:347
  115.8 8.3 %collective-permute-done.20.second_ref = bf16[32,16,512]{2,1,0:T(8,128)(2,1)S(1)} collective-permute-done((bf16[32,16,512]{2,1,0:T(8,128)(2,1)S(1)}, bf16[32,16,512]{2,1,0:T(8,128)(2,1)S(1)}, u32[]{:S(2)}, u32[]{:S(2)}) %collective-permute-start.20) | collective-permute-done | bytes 524320 | tf_op jit(solution)/shard_map/ppermute | solution.py:36
  124.0 14.7 %second_pair.1 = (bf16[32,16,512]{2,1,0:T(8,128)(2,1)S(1)}, bf16[256,4096]{1,0:T(8,128)(2,1)S(1)}, bf16[256,1024]{1,0:T(8,128)(2,1)S(1)}) custom-call(s32[1]{0:T(128)} %bitcast.section_ref, s32[64]{0:T(128)S(1)} %copy-done.4, bf16[32,16,512]{2,1,0:T(8,128)(2,1)S(1)} %collective-permute-done.20.second_ref, ...), custom_call_target="tpu_custom_call" | custom-call | tf_op jit(solution)/shard_map/second_pair/pallas_call | solution.py:435
  140.3 34.8 %collective-permute-done.22.given_ref = bf16[32,16,512]{2,1,0:T(8,128)(2,1)S(1)} collective-permute-done((bf16[32,16,512]{2,1,0:T(8,128)(2,1)S(1)}, bf16[32,16,512]{2,1,0:T(8,128)(2,1)S(1)}, u32[]{:S(2)}, u32[]{:S(2)}) %collective-permute-start.22) | collective-permute-done | bytes 524320 | tf_op jit(solution)/shard_map/ppermute | solution.py:40
  175.0 12.4 %back_first_pair.1 = (bf16[256,2048]{1,0:T(8,128)(2,1)S(1)}, bf16[256,2048]{1,0:T(8,128)(2,1)S(1)}, bf16[256,1024]{1,0:T(8,128)(2,1)S(1)}) custom-call(s32[1]{0:T(128)} %bitcast.section_ref, bf16[32,16,512]{2,1,0:T(8,128)(2,1)S(1)} %collective-permute-done.22.given_ref, bf16[32,16,512]{2,1,0:T(8,128)(2,1)S(1)} %get-tuple-element.51.skip_ref, ...), custom_call_target="tpu_custom_call" | custom-call | tf_op jit(solution)/shard_map/back_first_pair/pallas_call | solution.py:517
  188.1 2.9 %collective-permute-done.24.other_ref = bf16[256,1024]{1,0:T(8,128)(2,1)S(1)} collective-permute-done((bf16[256,1024]{1,0:T(8,128)(2,1)S(1)}, bf16[256,1024]{1,0:T(8,128)(2,1)S(1)}, u32[]{:S(2)}, u32[]{:S(2)}) %collective-permute-start.24) | collective-permute-done | bytes 524320 | tf_op jit(solution)/shard_map/ppermute | solution.py:23
  191.0 2.4 shard_map.60
  195.1 8.7 %collective-permute-start.26 = (bf16[2,512,256]{2,1,0:T(8,128)(2,1)S(1)}, bf16[2,512,256]{2,1,0:T(8,128)(2,1)S(1)}, u32[]{:S(2)}, u32[]{:S(2)}) collective-permute-start(bf16[2,512,256]{2,1,0:T(8,128)(2,1)S(1)} %get-tuple-element.76), channel_id=1, source_target_pairs={{0,24},{1,25},{2,26},{3,27},{4,28},{5,29},{6,30},{7,31},{8,16},{9,... | collective-permute-start | bytes 1572872 | tf_op jit(solution)/shard_map/ppermute | solution.py:23
  207.4 8.6 %collective-permute-done.26.refs_5_ = bf16[2,512,256]{2,1,0:T(8,128)(2,1)S(1)} collective-permute-done((bf16[2,512,256]{2,1,0:T(8,128)(2,1)S(1)}, bf16[2,512,256]{2,1,0:T(8,128)(2,1)S(1)}, u32[]{:S(2)}, u32[]{:S(2)}) %collective-permute-start.26) | collective-permute-done | bytes 524320 | tf_op jit(solution)/shard_map/ppermute | solution.py:23
  221.6 3.0 %collective-permute-start.31 = (bf16[512,256]{1,0:T(8,128)(2,1)S(1)}, bf16[512,256]{1,0:T(8,128)(2,1)S(1)}, u32[]{:S(2)}, u32[]{:S(2)}) collective-permute-start(bf16[512,256]{1,0:T(8,128)(2,1)S(1)} %get-tuple-element.85), channel_id=1, source_target_pairs={{0,6},{1,7},{2,4},{3,5},{4,2},{5,3},{6,0},{7,1},{8,14},{9,15},{10,... | collective-permute-start | bytes 786440 | tf_op jit(solution)/shard_map/ppermute | solution.py:23
  224.6 3.0 %collective-permute-done.29.refs_4_ = bf16[512,256]{1,0:T(8,128)(2,1)S(1)} collective-permute-done((bf16[512,256]{1,0:T(8,128)(2,1)S(1)}, bf16[512,256]{1,0:T(8,128)(2,1)S(1)}, u32[]{:S(2)}, u32[]{:S(2)}) %collective-permute-start.29) | collective-permute-done | bytes 262176 | tf_op jit(solution)/shard_map/ppermute | solution.py:23
  231.6 2.9 %collective-permute-start.34 = (bf16[128,512]{1,0:T(8,128)(2,1)S(1)}, bf16[128,512]{1,0:T(8,128)(2,1)S(1)}, u32[]{:S(2)}, u32[]{:S(2)}) collective-permute-start(bf16[128,512]{1,0:T(8,128)(2,1)S(1)} %get-tuple-element.90), channel_id=1, source_target_pairs={{0,4},{1,5},{2,6},{3,7},{4,0},{5,1},{6,2},{7,3},{8,12},{9,13},{10,... | collective-permute-start | bytes 393224 | tf_op jit(solution)/shard_map/ppermute | solution.py:23
  238.7 2.2 collective-permute-start.38
  241.1 3.3 %collective-permute-done.37.refs_6_ = bf16[128,512]{1,0:T(8,128)(2,1)S(1)} collective-permute-done((bf16[128,512]{1,0:T(8,128)(2,1)S(1)}, bf16[128,512]{1,0:T(8,128)(2,1)S(1)}, u32[]{:S(2)}, u32[]{:S(2)}) %collective-permute-start.37) | collective-permute-done | bytes 131104 | tf_op jit(solution)/shard_map/ppermute | solution.py:23
  245.9 2.1 collective-permute-start.39
  248.0 6.8 %collective-permute-done.39 = bf16[64,1024]{1,0:T(8,128)(2,1)S(1)} collective-permute-done((bf16[64,1024]{1,0:T(8,128)(2,1)S(1)}, bf16[64,1024]{1,0:T(8,128)(2,1)S(1)}, u32[]{:S(2)}, u32[]{:S(2)}) %collective-permute-start.39) | collective-permute-done | bytes 131104 | tf_op jit(solution)/shard_map/ppermute | solution.py:23
  (102 shorter events, 56.5 us)
Async XLA Ops:
  2.9 8.4 %collective-permute-start.4 = (bf16[128,1024]{1,0:T(8,128)(2,1)}, bf16[128,1024]{1,0:T(8,128)(2,1)S(1)}, u32[]{:S(2)}, u32[]{:S(2)}) collective-permute-start(bf16[128,1024]{1,0:T(8,128)(2,1)} %shard_map.55), channel_id=1, source_target_pairs={{0,64},{64,0},{128,192},{192,128},{1,65},{65,1},{129,193},{193,129... | collective-permute-start | bytes 786440 | tf_op jit(solution)/shard_map/ppermute | solution.py:27
  11.4 8.7 %collective-permute-start.7 = (bf16[128,512]{1,0:T(8,128)(2,1)S(1)}, bf16[128,512]{1,0:T(8,128)(2,1)S(1)}, u32[]{:S(2)}, u32[]{:S(2)}) collective-permute-start(bf16[128,512]{1,0:T(8,128)(2,1)S(1)} %get-tuple-element.52.refs_0_), channel_id=1, source_target_pairs={{0,24},{1,25},{2,26},{3,27},{4,28},{5,29},{6,30},{7,31},{8,16},{9,... | collective-permute-start | bytes 393224 | tf_op jit(solution)/shard_map/ppermute | solution.py:23
  11.9 9.7 %collective-permute-start.6 = (bf16[128,512]{1,0:T(8,128)(2,1)S(1)}, bf16[128,512]{1,0:T(8,128)(2,1)S(1)}, u32[]{:S(2)}, u32[]{:S(2)}) collective-permute-start(bf16[128,512]{1,0:T(8,128)(2,1)S(1)} %get-tuple-element.52.refs_0_), channel_id=1, source_target_pairs={{0,16},{1,17},{2,18},{3,19},{4,20},{5,21},{6,22},{7,23},{8,24},{9,... | collective-permute-start | bytes 393224 | tf_op jit(solution)/shard_map/ppermute | solution.py:23
  14.3 7.3 %collective-permute-start.5 = (bf16[128,512]{1,0:T(8,128)(2,1)S(1)}, bf16[128,512]{1,0:T(8,128)(2,1)S(1)}, u32[]{:S(2)}, u32[]{:S(2)}) collective-permute-start(bf16[128,512]{1,0:T(8,128)(2,1)S(1)} %get-tuple-element.52.refs_0_), channel_id=1, source_target_pairs={{0,8},{1,9},{2,10},{3,11},{4,12},{5,13},{6,14},{7,15},{8,0},{9,1},... | collective-permute-start | bytes 393224 | tf_op jit(solution)/shard_map/ppermute | solution.py:23
  15.5 7.6 %collective-permute-start.10 = (bf16[128,512]{1,0:T(8,128)(2,1)S(1)}, bf16[128,512]{1,0:T(8,128)(2,1)S(1)}, u32[]{:S(2)}, u32[]{:S(2)}) collective-permute-start(bf16[128,512]{1,0:T(8,128)(2,1)S(1)} %get-tuple-element.53.refs_1_), channel_id=1, source_target_pairs={{0,6},{1,7},{2,4},{3,5},{4,2},{5,3},{6,0},{7,1},{8,14},{9,15},{10,... | collective-permute-start | bytes 393224 | tf_op jit(solution)/shard_map/ppermute | solution.py:23
  18.5 7.0 %collective-permute-start.9 = (bf16[128,512]{1,0:T(8,128)(2,1)S(1)}, bf16[128,512]{1,0:T(8,128)(2,1)S(1)}, u32[]{:S(2)}, u32[]{:S(2)}) collective-permute-start(bf16[128,512]{1,0:T(8,128)(2,1)S(1)} %get-tuple-element.53.refs_1_), channel_id=1, source_target_pairs={{0,4},{1,5},{2,6},{3,7},{4,0},{5,1},{6,2},{7,3},{8,12},{9,13},{10,... | collective-permute-start | bytes 393224 | tf_op jit(solution)/shard_map/ppermute | solution.py:23
  25.6 14.1 %collective-permute-start.13 = (bf16[512,512]{1,0:T(8,128)(2,1)S(1)}, bf16[512,512]{1,0:T(8,128)(2,1)S(1)}, u32[]{:S(2)}, u32[]{:S(2)}) collective-permute-start(bf16[512,512]{1,0:T(8,128)(2,1)S(1)} %get-tuple-element.54.refs_0_), channel_id=1, source_target_pairs={{0,6},{1,7},{2,4},{3,5},{4,2},{5,3},{6,0},{7,1},{8,14},{9,15},{10,... | collective-permute-start | bytes 1572872 | tf_op jit(solution)/shard_map/ppermute | solution.py:23
  28.6 12.6 %collective-permute-start.11 = (bf16[512,512]{1,0:T(8,128)(2,1)S(1)}, bf16[512,512]{1,0:T(8,128)(2,1)S(1)}, u32[]{:S(2)}, u32[]{:S(2)}) collective-permute-start(bf16[512,512]{1,0:T(8,128)(2,1)S(1)} %get-tuple-element.54.refs_0_), channel_id=1, source_target_pairs={{0,2},{1,3},{2,0},{3,1},{4,6},{5,7},{6,4},{7,5},{8,10},{9,11},{10,... | collective-permute-start | bytes 1572872 | tf_op jit(solution)/shard_map/ppermute | solution.py:23
  28.7 13.7 %collective-permute-start.14 = (bf16[512,512]{1,0:T(8,128)(2,1)S(1)}, bf16[512,512]{1,0:T(8,128)(2,1)S(1)}, u32[]{:S(2)}, u32[]{:S(2)}) collective-permute-start(bf16[512,512]{1,0:T(8,128)(2,1)S(1)} %get-tuple-element.55.refs_1_), channel_id=1, source_target_pairs={{0,24},{1,25},{2,26},{3,27},{4,28},{5,29},{6,30},{7,31},{8,16},{9,... | collective-permute-start | bytes 1572872 | tf_op jit(solution)/shard_map/ppermute | solution.py:23
  28.7 13.7 %collective-permute-start.12 = (bf16[512,512]{1,0:T(8,128)(2,1)S(1)}, bf16[512,512]{1,0:T(8,128)(2,1)S(1)}, u32[]{:S(2)}, u32[]{:S(2)}) collective-permute-start(bf16[512,512]{1,0:T(8,128)(2,1)S(1)} %get-tuple-element.55.refs_1_), channel_id=1, source_target_pairs={{0,8},{1,9},{2,10},{3,11},{4,12},{5,13},{6,14},{7,15},{8,0},{9,1},... | collective-permute-start | bytes 1572872 | tf_op jit(solution)/shard_map/ppermute | solution.py:23
  44.3 7.6 %collective-permute-start.17 = (bf16[512,256]{1,0:T(8,128)(2,1)S(1)}, bf16[512,256]{1,0:T(8,128)(2,1)S(1)}, u32[]{:S(2)}, u32[]{:S(2)}) collective-permute-start(bf16[512,256]{1,0:T(8,128)(2,1)S(1)} %get-tuple-element.58), channel_id=1, source_target_pairs={{0,6},{1,7},{2,4},{3,5},{4,2},{5,3},{6,0},{7,1},{8,14},{9,15},{10,... | collective-permute-start | bytes 786440 | tf_op jit(solution)/shard_map/ppermute | solution.py:23
  44.6 7.6 %collective-permute-start.18 = (bf16[512,256]{1,0:T(8,128)(2,1)S(1)}, bf16[512,256]{1,0:T(8,128)(2,1)S(1)}, u32[]{:S(2)}, u32[]{:S(2)}) collective-permute-start(bf16[512,256]{1,0:T(8,128)(2,1)S(1)} %get-tuple-element.59), channel_id=1, source_target_pairs={{0,24},{1,25},{2,26},{3,27},{4,28},{5,29},{6,30},{7,31},{8,16},{9,... | collective-permute-start | bytes 786440 | tf_op jit(solution)/shard_map/ppermute | solution.py:23
  54.6 43.1 %collective-permute-start.19 = (bf16[2048,1024]{1,0:T(8,128)(2,1)}, bf16[2048,1024]{1,0:T(8,128)(2,1)}, u32[]{:S(2)}, u32[]{:S(2)}) collective-permute-start(bf16[2048,1024]{1,0:T(8,128)(2,1)} %shard_map.59.near_ref), channel_id=1, source_target_pairs={{0,1},{1,0},{2,3},{3,2},{4,5},{5,4},{6,7},{7,6},{8,9},{9,8},{10,11... | collective-permute-start | bytes 12582920 | tf_op jit(solution)/shard_map/ppermute | solution.py:23
  54.6 16.8 %collective-permute-start = (bf16[24,32,256]{2,1,0:T(8,128)(2,1)S(1)}, bf16[24,32,256]{2,1,0:T(8,128)(2,1)S(1)}, u32[]{:S(2)}, u32[]{:S(2)}) collective-permute-start(bf16[24,32,256]{2,1,0:T(8,128)(2,1)S(1)} %copy-done.7), channel_id=1, source_target_pairs={{0,224},{1,225},{2,226},{3,227},{4,228},{5,229},{6,230},{7,231},{8... | collective-permute-start | bytes 1179656 | tf_op jit(solution)/shard_map/ppermute | solution.py:629
  62.4 28.2 %collective-permute-start.3 = (bf16[2304,256]{1,0:T(8,128)(2,1)S(1)}, bf16[2304,256]{1,0:T(8,128)(2,1)S(1)}, u32[]{:S(2)}, u32[]{:S(2)}) collective-permute-start(bf16[2304,256]{1,0:T(8,128)(2,1)S(1)} %bitcast.7), channel_id=1, source_target_pairs={{0,64},{64,0},{128,192},{192,128},{1,65},{65,1},{129,193},{193,129... | collective-permute-start | bytes 3538952 | tf_op jit(solution)/shard_map/ppermute | solution.py:27
  73.2 9.0 %collective-permute-start.2 = (f32[8,16,512]{2,1,0:T(8,128)}, f32[8,16,512]{2,1,0:T(8,128)}, u32[]{:S(2)}, u32[]{:S(2)}) collective-permute-start(f32[8,16,512]{2,1,0:T(8,128)} %select_n.73), channel_id=1, source_target_pairs={{0,1},{4,5},{8,9},{12,13},{16,17},{20,21},{24,25},{28,29},{32,33},... | collective-permute-start | bytes 786440 | tf_op jit(solution)/shard_map/ppermute | solution.py:638
  76.5 12.9 %collective-permute-start.1 = (f32[16,16,512]{2,1,0:T(8,128)}, f32[16,16,512]{2,1,0:T(8,128)}, u32[]{:S(2)}, u32[]{:S(2)}) collective-permute-start(f32[16,16,512]{2,1,0:T(8,128)} %slice.15), channel_id=1, source_target_pairs={{3,4},{7,8},{11,12},{15,16},{19,20},{23,24},{27,28},{31,32},{35,36... | collective-permute-start | bytes 1572872 | tf_op jit(solution)/shard_map/ppermute | solution.py:634
  93.3 22.5 %collective-permute-start.21 = (bf16[32,16,512]{2,1,0:T(8,128)(2,1)S(1)}, bf16[32,16,512]{2,1,0:T(8,128)(2,1)S(1)}, u32[]{:S(2)}, u32[]{:S(2)}) collective-permute-start(bf16[32,16,512]{2,1,0:T(8,128)(2,1)S(1)} %get-tuple-element.51.skip_ref), channel_id=1, source_target_pairs={{64,128},{65,129},{66,130},{67,131},{68,132},{69,133},{70,134},{71... | collective-permute-start | bytes 1572872 | tf_op jit(solution)/shard_map/ppermute | solution.py:36
  114.4 9.6 %collective-permute-start.20 = (bf16[32,16,512]{2,1,0:T(8,128)(2,1)S(1)}, bf16[32,16,512]{2,1,0:T(8,128)(2,1)S(1)}, u32[]{:S(2)}, u32[]{:S(2)}) collective-permute-start(bf16[32,16,512]{2,1,0:T(8,128)(2,1)S(1)} %get-tuple-element.60), channel_id=1, source_target_pairs={{64,128},{65,129},{66,130},{67,131},{68,132},{69,133},{70,134},{71... | collective-permute-start | bytes 1572872 | tf_op jit(solution)/shard_map/ppermute | solution.py:36
  138.7 36.3 %collective-permute-start.22 = (bf16[32,16,512]{2,1,0:T(8,128)(2,1)S(1)}, bf16[32,16,512]{2,1,0:T(8,128)(2,1)S(1)}, u32[]{:S(2)}, u32[]{:S(2)}) collective-permute-start(bf16[32,16,512]{2,1,0:T(8,128)(2,1)S(1)} %get-tuple-element.62), channel_id=1, source_target_pairs={{128,64},{129,65},{130,66},{131,67},{132,68},{133,69},{134,70},{13... | collective-permute-start | bytes 1572872 | tf_op jit(solution)/shard_map/ppermute | solution.py:40
  193.4 14.0 %collective-permute-start.25 = (bf16[2,512,256]{2,1,0:T(8,128)(2,1)S(1)}, bf16[2,512,256]{2,1,0:T(8,128)(2,1)S(1)}, u32[]{:S(2)}, u32[]{:S(2)}) collective-permute-start(bf16[2,512,256]{2,1,0:T(8,128)(2,1)S(1)} %get-tuple-element.75), channel_id=1, source_target_pairs={{0,8},{1,9},{2,10},{3,11},{4,12},{5,13},{6,14},{7,15},{8,0},{9,1},... | collective-permute-start | bytes 1572872 | tf_op jit(solution)/shard_map/ppermute | solution.py:23
  195.1 20.9 %collective-permute-start.26 = (bf16[2,512,256]{2,1,0:T(8,128)(2,1)S(1)}, bf16[2,512,256]{2,1,0:T(8,128)(2,1)S(1)}, u32[]{:S(2)}, u32[]{:S(2)}) collective-permute-start(bf16[2,512,256]{2,1,0:T(8,128)(2,1)S(1)} %get-tuple-element.76), channel_id=1, source_target_pairs={{0,24},{1,25},{2,26},{3,27},{4,28},{5,29},{6,30},{7,31},{8,16},{9,... | collective-permute-start | bytes 1572872 | tf_op jit(solution)/shard_map/ppermute | solution.py:23
  203.8 13.7 %collective-permute-start.27 = (bf16[2,512,256]{2,1,0:T(8,128)(2,1)S(1)}, bf16[2,512,256]{2,1,0:T(8,128)(2,1)S(1)}, u32[]{:S(2)}, u32[]{:S(2)}) collective-permute-start(bf16[2,512,256]{2,1,0:T(8,128)(2,1)S(1)} %get-tuple-element.77), channel_id=1, source_target_pairs={{0,2},{1,3},{2,0},{3,1},{4,6},{5,7},{6,4},{7,5},{8,10},{9,11},{10,... | collective-permute-start | bytes 1572872 | tf_op jit(solution)/shard_map/ppermute | solution.py:23
  203.8 14.9 %collective-permute-start.28 = (bf16[2,512,256]{2,1,0:T(8,128)(2,1)S(1)}, bf16[2,512,256]{2,1,0:T(8,128)(2,1)S(1)}, u32[]{:S(2)}, u32[]{:S(2)}) collective-permute-start(bf16[2,512,256]{2,1,0:T(8,128)(2,1)S(1)} %get-tuple-element.78), channel_id=1, source_target_pairs={{0,6},{1,7},{2,4},{3,5},{4,2},{5,3},{6,0},{7,1},{8,14},{9,15},{10,... | collective-permute-start | bytes 1572872 | tf_op jit(solution)/shard_map/ppermute | solution.py:23
  219.1 8.5 %collective-permute-start.29 = (bf16[512,256]{1,0:T(8,128)(2,1)S(1)}, bf16[512,256]{1,0:T(8,128)(2,1)S(1)}, u32[]{:S(2)}, u32[]{:S(2)}) collective-permute-start(bf16[512,256]{1,0:T(8,128)(2,1)S(1)} %get-tuple-element.83), channel_id=1, source_target_pairs={{0,24},{1,25},{2,26},{3,27},{4,28},{5,29},{6,30},{7,31},{8,16},{9,... | collective-permute-start | bytes 786440 | tf_op jit(solution)/shard_map/ppermute | solution.py:23
  221.2 7.5 %collective-permute-start.30 = (bf16[512,256]{1,0:T(8,128)(2,1)S(1)}, bf16[512,256]{1,0:T(8,128)(2,1)S(1)}, u32[]{:S(2)}, u32[]{:S(2)}) collective-permute-start(bf16[512,256]{1,0:T(8,128)(2,1)S(1)} %get-tuple-element.84), channel_id=1, source_target_pairs={{0,8},{1,9},{2,10},{3,11},{4,12},{5,13},{6,14},{7,15},{8,0},{9,1},... | collective-permute-start | bytes 786440 | tf_op jit(solution)/shard_map/ppermute | solution.py:23
  221.6 8.3 %collective-permute-start.31 = (bf16[512,256]{1,0:T(8,128)(2,1)S(1)}, bf16[512,256]{1,0:T(8,128)(2,1)S(1)}, u32[]{:S(2)}, u32[]{:S(2)}) collective-permute-start(bf16[512,256]{1,0:T(8,128)(2,1)S(1)} %get-tuple-element.85), channel_id=1, source_target_pairs={{0,6},{1,7},{2,4},{3,5},{4,2},{5,3},{6,0},{7,1},{8,14},{9,15},{10,... | collective-permute-start | bytes 786440 | tf_op jit(solution)/shard_map/ppermute | solution.py:23
  231.2 7.5 %collective-permute-start.33 = (bf16[128,512]{1,0:T(8,128)(2,1)S(1)}, bf16[128,512]{1,0:T(8,128)(2,1)S(1)}, u32[]{:S(2)}, u32[]{:S(2)}) collective-permute-start(bf16[128,512]{1,0:T(8,128)(2,1)S(1)} %get-tuple-element.89), channel_id=1, source_target_pairs={{0,2},{1,3},{2,0},{3,1},{4,6},{5,7},{6,4},{7,5},{8,10},{9,11},{10,... | collective-permute-start | bytes 393224 | tf_op jit(solution)/shard_map/ppermute | solution.py:23
  231.6 9.3 %collective-permute-start.34 = (bf16[128,512]{1,0:T(8,128)(2,1)S(1)}, bf16[128,512]{1,0:T(8,128)(2,1)S(1)}, u32[]{:S(2)}, u32[]{:S(2)}) collective-permute-start(bf16[128,512]{1,0:T(8,128)(2,1)S(1)} %get-tuple-element.90), channel_id=1, source_target_pairs={{0,4},{1,5},{2,6},{3,7},{4,0},{5,1},{6,2},{7,3},{8,12},{9,13},{10,... | collective-permute-start | bytes 393224 | tf_op jit(solution)/shard_map/ppermute | solution.py:23
  237.9 6.6 %collective-permute-start.37 = (bf16[128,512]{1,0:T(8,128)(2,1)S(1)}, bf16[128,512]{1,0:T(8,128)(2,1)S(1)}, u32[]{:S(2)}, u32[]{:S(2)}) collective-permute-start(bf16[128,512]{1,0:T(8,128)(2,1)S(1)} %get-tuple-element.93), channel_id=1, source_target_pairs={{0,16},{1,17},{2,18},{3,19},{4,20},{5,21},{6,22},{7,23},{8,24},{9,... | collective-permute-start | bytes 393224 | tf_op jit(solution)/shard_map/ppermute | solution.py:23
  238.7 7.1 %collective-permute-start.38 = (bf16[128,512]{1,0:T(8,128)(2,1)S(1)}, bf16[128,512]{1,0:T(8,128)(2,1)S(1)}, u32[]{:S(2)}, u32[]{:S(2)}) collective-permute-start(bf16[128,512]{1,0:T(8,128)(2,1)S(1)} %get-tuple-element.94), channel_id=1, source_target_pairs={{0,24},{1,25},{2,26},{3,27},{4,28},{5,29},{6,30},{7,31},{8,16},{9,... | collective-permute-start | bytes 393224 | tf_op jit(solution)/shard_map/ppermute | solution.py:23
  245.9 9.0 %collective-permute-start.39 = (bf16[64,1024]{1,0:T(8,128)(2,1)S(1)}, bf16[64,1024]{1,0:T(8,128)(2,1)S(1)}, u32[]{:S(2)}, u32[]{:S(2)}) collective-permute-start(bf16[64,1024]{1,0:T(8,128)(2,1)S(1)} %get-tuple-element.96), channel_id=1, source_target_pairs={{0,32},{1,33},{2,34},{3,35},{4,36},{5,37},{6,38},{7,39},{8,40},{9,... | collective-permute-start | bytes 393224 | tf_op jit(solution)/shard_map/ppermute | solution.py:23
  (20 other events, 186.9 us)
